TPU v7x, 256 devices: a whole 4x4x8 slice. The times are simulated.
256 devices in a mesh: dp: 8 (over x, z_hi), ctx: 32 (over y, z_lo, core).
Axes of the slice: x: 4, y: 4, z: 8 (z_hi: 2, z_lo: 4; z = z_hi * 4 + z_lo), core: 2. Of those that a mesh axis runs over, the one named last changes fastest.
Arguments:
- layer_input: bfloat16 [8, 4096, 8192], P('dp', 'ctx'), may hold values from -6 to 6
- queries: bfloat16 [8, 4096, 1024], P('dp', 'ctx'), may hold values from -6 to 6
- keys: bfloat16 [8, 4096, 128], P('dp', 'ctx'), may hold values from -6 to 6
- values: bfloat16 [8, 4096, 128], P('dp', 'ctx'), may hold values from -6 to 6
- d_out: bfloat16 [8, 4096, 1024], P('dp', 'ctx'), may hold values from -6 to 6
- doc_lengths: int32 [8, 8], P('dp'), may hold values from 1 to 1024, 4096 in all within a row
- block_order: int32 [64], replicated, may hold values from 0 to 63, as said below
Outputs:
- query_grad: bfloat16 [8, 4096, 1024], P('dp', 'ctx')
- key_grad: bfloat16 [8, 4096, 128], P('dp', 'ctx')
- value_grad: bfloat16 [8, 4096, 128], P('dp', 'ctx')
- kv_weight_grad: float32 [32, 256, 256], P('ctx', 'dp')
Inputs may be any that keep to these rules, and one draw needn't show every extreme that they name: `block_order`: entries 2r and 2r+1 are the blocks stored in rows 2r*64 to 2r*64 + 2*64 - 1; they sum to 63, and every block appears once.
All inputs are finite; a program needn't handle non-finite values.
Results may differ from a plain program's by a relative error of at most 0.012.
Values may be sent and summed in bfloat16 or wider, within the bound.
A program may use at most 64 MiB of HBM per device.

v0:
```python
import math
import jax
import jax.numpy as jnp
from jax import lax
from jax.sharding import PartitionSpec as P

big_negative = -1e30


def per_device(layer_input, queries, keys, values, d_out, doc_lengths, block_order):
    local_len = queries.shape[1]
    head_dim = keys.shape[2]
    heads = queries.shape[2] // head_dim
    ctx_size = lax.axis_size("ctx")
    seq_len = local_len * ctx_size
    half = local_len // 2
    rank = lax.axis_index("ctx")
    scale = 1.0 / math.sqrt(head_dim)
    key_pos = (block_order[:, None] * half + jnp.arange(half, dtype=jnp.int32)[None, :]).reshape(
        seq_len
    )
    ends = jnp.cumsum(doc_lengths[0])
    key_doc = jnp.sum((key_pos[:, None] >= ends[None, :]).astype(jnp.int32), axis=1)
    query_pos = lax.dynamic_slice_in_dim(key_pos, rank * local_len, local_len)
    query_doc = lax.dynamic_slice_in_dim(key_doc, rank * local_len, local_len)
    local_rows = layer_input[0]
    all_keys, all_values = (
        lax.all_gather(keys[0], "ctx", axis=0, tiled=True),
        lax.all_gather(values[0], "ctx", axis=0, tiled=True),
    )
    block = 512
    nblocks = seq_len // block
    key_blocks = all_keys.reshape(nblocks, block, head_dim)
    value_blocks = all_values.reshape(nblocks, block, head_dim)
    pos_blocks = key_pos.reshape(nblocks, block)
    doc_blocks = key_doc.reshape(nblocks, block)
    q_heads = queries[0].reshape(local_len, heads, head_dim)
    d_heads = d_out[0].reshape(local_len, heads, head_dim)

    def visible(kpos, kdoc):
        return ((kpos[None, :] <= query_pos[:, None]) & (kdoc[None, :] == query_doc[:, None]))[None]

    def scores(kblock):
        return (
            jnp.einsum("thd,kd->htk", q_heads, kblock, preferred_element_type=jnp.float32) * scale
        )

    def prob_grads(vblock):
        return jnp.einsum("thd,kd->htk", d_heads, vblock, preferred_element_type=jnp.float32)

    def stats_step(carry, item):
        run_max, run_sum, run_dot = carry
        kblock, vblock, kpos, kdoc = item
        mask = visible(kpos, kdoc)
        s = scores(kblock)
        new_max = jnp.maximum(run_max, jnp.max(jnp.where(mask, s, big_negative), axis=2))
        terms = jnp.where(mask, jnp.exp(s - new_max[..., None]), 0.0)
        factor = jnp.exp(run_max - new_max)
        run_sum = run_sum * factor + jnp.sum(terms, axis=2)
        run_dot = run_dot * factor + jnp.sum(terms * prob_grads(vblock), axis=2)
        return ((new_max, run_sum, run_dot), None)

    items = (key_blocks, value_blocks, pos_blocks, doc_blocks)
    zeros_stat = jnp.zeros((heads, local_len), jnp.float32)
    start_stats = (jnp.full((heads, local_len), big_negative, jnp.float32), zeros_stat, zeros_stat)
    (run_max, run_sum, run_dot), _ = lax.scan(stats_step, start_stats, items)
    lse = run_max + jnp.log(run_sum)
    delta = run_dot / run_sum

    def grad_step(dq_acc, item):
        kblock, vblock, kpos, kdoc = item
        p = jnp.where(visible(kpos, kdoc), jnp.exp(scores(kblock) - lse[..., None]), 0.0)
        weights = p.astype(jnp.bfloat16)
        dprob = prob_grads(vblock)
        dscore = (p * (dprob - delta[..., None])).astype(jnp.bfloat16)
        dq_acc = dq_acc + jnp.einsum(
            "htk,kd->thd", dscore, kblock, preferred_element_type=jnp.float32
        )
        dk_part = (
            jnp.einsum("htk,thd->kd", dscore, q_heads, preferred_element_type=jnp.float32) * scale
        )
        dv_part = jnp.einsum("htk,thd->kd", weights, d_heads, preferred_element_type=jnp.float32)
        return (dq_acc, jnp.concatenate([dk_part, dv_part], axis=1))

    dq_acc, partials = lax.scan(
        grad_step, jnp.zeros((local_len, heads, head_dim), jnp.float32), items
    )
    owned = lax.psum_scatter(
        partials.reshape(seq_len, 2 * head_dim), "ctx", scatter_dimension=0, tiled=True
    )
    kv_grad = owned.astype(jnp.bfloat16)
    query_grad = (dq_acc * scale).astype(jnp.bfloat16).reshape(1, local_len, heads * head_dim)
    contract = (((0,), (0,)), ((), ()))
    exact = lax.Precision.HIGHEST
    cols = local_rows.astype(jnp.float32)
    term = lax.psum_scatter(
        lax.dot_general(cols, owned, contract, precision=exact, preferred_element_type=jnp.float32),
        "ctx",
        scatter_dimension=0,
        tiled=True,
    )
    weight_grad = lax.psum_scatter(term, "dp", scatter_dimension=0, tiled=True)
    weight_grad = weight_grad * (1.0 / math.sqrt(lax.axis_size("dp") * seq_len))
    key_grad = kv_grad[:, :head_dim].reshape(1, local_len, head_dim)
    value_grad = kv_grad[:, head_dim:].reshape(1, local_len, head_dim)
    return (
        query_grad,
        key_grad,
        value_grad,
        weight_grad.reshape(1, weight_grad.shape[0], 2 * head_dim),
    )


def solution(mesh):
    placed = (
        P("dp", "ctx", None),
        P("dp", "ctx", None),
        P("dp", "ctx", None),
        P("dp", "ctx", None),
        P("dp", "ctx", None),
        P("dp", None),
        P(),
    )
    return jax.shard_map(
        per_device,
        mesh=mesh,
        in_specs=placed,
        out_specs=(
            P("dp", "ctx", None),
            P("dp", "ctx", None),
            P("dp", "ctx", None),
            P("ctx", "dp", None),
        ),
        check_vma=False,
    )
```

profile of v0, /device:TPU:8, one launch (start us, length us, event | category | flops | bytes accessed | tf_op | source)
XLA Modules:
  0.0 636.3 jit_solution(2492663735038133514)
XLA Ops:
  11.0 1.8 copy.43
  15.2 56.2 %all-gather.5.cloned.1.call-done = bf16[1,4096,128]{2,1,0:T(8,128)(2,1)} async-done(((bf16[1,128,128]{2,1,0:T(8,128)(2,1)}), bf16[1,4096,128]{2,1,0:T(8,128)(2,1)}) %all-gather.5.cloned.1.call-update) | async-done | bytes 1048592 | tf_op jit(solution)/shard_map/all_gather | solution.py:28
  71.4 59.7 %all-gather.7.cloned.1.call-done = bf16[1,4096,128]{2,1,0:T(8,128)(2,1)} async-done(((bf16[1,128,128]{2,1,0:T(8,128)(2,1)}), bf16[1,4096,128]{2,1,0:T(8,128)(2,1)}) %all-gather.7.cloned.1.call-update) | async-done | bytes 1048592 | tf_op jit(solution)/shard_map/all_gather | solution.py:29
  131.1 29.4 %while.28 = (s32[]{:T(128)}, f32[8,128]{1,0:T(8,128)S(1)}, f32[8,128]{1,0:T(8,128)S(1)}, f32[8,128]{1,0:T(8,128)S(1)}, s32[8,512]{1,0:T(8,128)S(1)}, /*index=5*/...) while((s32[]{:T(128)}, f32[8,128]{1,0:T(8,128)S(1)}, ...), condition=%wide.region_6.7_spmd.clone, body=%wide.region_2.6_spmd.clone.sunk | while | flops 274930688 | bytes 7427236 | solution.py:66
  132.7 1.6 fusion.66
  136.4 1.6 fusion.66
  140.0 1.6 fusion.66
  143.7 1.6 fusion.66
  147.4 1.6 fusion.66
  151.0 1.6 fusion.66
  160.5 67.4 %while.29 = (s32[]{:T(128)}, f32[128,8,128]{0,2,1:T(8,128)}, f32[8,512,256]{2,1,0:T(8,128)}, bf16[8,512,128]{2,1,0:T(8,128)(2,1)}, s32[8,512]{1,0:T(8,128)S(1)},...) while((s32[]{:T(128)}, f32[128,8,128]{0,2,1:T(8,128)}, ...), condition=%wide.region_8.9_spmd.clone, body=%wide.region_7.8_spmd.clone.sunk | while | flops 675414016 | bytes 15750323 | solution.py:85
  160.7 1.6 fusion.79
  165.5 2.1 fusion.81
  168.9 1.6 fusion.79
  173.7 2.3 fusion.81
  177.3 1.6 fusion.79
  182.2 2.3 fusion.81
  185.8 1.6 fusion.79
  190.6 2.3 fusion.81
  194.3 1.6 fusion.79
  199.1 2.3 fusion.81
  202.7 1.6 fusion.79
  207.5 2.3 fusion.81
  211.1 1.6 fusion.79
  216.0 2.3 fusion.81
  219.6 1.6 fusion.79
  224.4 2.3 fusion.81
  227.9 131.9 %reduce-scatter.6.cloned.1.call-done = f32[128,256]{1,0:T(8,128)} async-done(((f32[4096,256]{1,0:T(8,128)}), f32[128,256]{1,0:T(8,128)}) %reduce-scatter.6.cloned.1.call-update) | async-done | bytes 131088 | tf_op jit(solution)/shard_map/reduce_scatter | solution.py:88
  359.8 6.6 %convolution_bitcast_fusion.3 = f32[8192,256]{0,1:T(8,128)} fusion(f32[128,256]{1,0:T(8,128)} %reduce-scatter.6.cloned.1.call-done, bf16[1,128,8192]{2,1,0:T(8,128)(2,1)S(1)} %copy-done), kind=kOutput, calls=%fused_computation.50 | convolution fusion | flops 3221225472 | bytes 10616832 | tf_op jit(solution)/shard_map/dot_general | solution.py:97
  366.5 159.5 %reduce-scatter.8.cloned.1.call-done = f32[256,256]{0,1:T(8,128)} async-done(((f32[8192,256]{0,1:T(8,128)}), f32[256,256]{0,1:T(8,128)}) %reduce-scatter.8.cloned.1.call-update) | async-done | bytes 262160 | tf_op jit(solution)/shard_map/reduce_scatter | solution.py:96
  526.0 1.8 copy.58
  530.3 97.8 %reduce-scatter.10.cloned.1.call-done = f32[32,256]{1,0:T(8,128)} async-done(((f32[256,256]{1,0:T(8,128)}), f32[32,256]{1,0:T(8,128)}) %reduce-scatter.10.cloned.1.call-update) | async-done | bytes 32784
  (166 shorter events, 65.9 us)
Async XLA Ops:
  7.2 352.6 %copy-start = (bf16[1,128,8192]{2,1,0:T(8,128)(2,1)S(1)}, bf16[1,128,8192]{2,1,0:T(8,128)(2,1)}, u32[]{:S(2)}) copy-start(bf16[1,128,8192]{2,1,0:T(8,128)(2,1)} %param.11) | copy-start | bytes 6291460
  7.2 64.2 %all-gather.5.cloned.1.call-start = ((), (), s32[]{:S(2)}) async-start(), calls=%async_computation.5 | async-start | bytes 1081344 | tf_op jit(solution)/shard_map/all_gather | solution.py:28
  7.9 123.2 %all-gather.7.cloned.1.call-start = ((), (), s32[]{:S(2)}) async-start(), calls=%async_computation.6 | async-start | bytes 1081344 | tf_op jit(solution)/shard_map/all_gather | solution.py:29
  8.7 351.1 %reduce-scatter.6.cloned.1.call-start = ((), (), s32[]{:S(2)}) async-start(), calls=%async_computation.3 | async-start | bytes 4325376 | tf_op jit(solution)/shard_map/reduce_scatter | solution.py:88
  227.8 298.1 %reduce-scatter.8.cloned.1.call-start = ((), (), s32[]{:S(2)}) async-start(), calls=%async_computation.4 | async-start | bytes 8650752 | tf_op jit(solution)/shard_map/reduce_scatter | solution.py:96
  366.4 163.3 %copy-start.1 = (f32[128,256]{1,0:T(8,128)S(1)}, f32[128,256]{1,0:T(8,128)}, u32[]{:S(2)}) copy-start(f32[128,256]{1,0:T(8,128)} %reduce-scatter.6.cloned.1.call-done) | copy-start | bytes 393220
  366.4 261.8 %reduce-scatter.10.cloned.1.call-start = ((), (), s32[]{:S(2)}) async-start(), calls=%async_computation.7 | async-start | bytes 294912
Sparse Core Ops, SparseCore 0:
  9.9 61.4 all-gather.4
  73.3 57.7 all-gather.6
  228.0 131.8 reduce-scatter.5
  366.5 159.3 reduce-scatter.7
  529.6 98.4 reduce-scatter.9
where the time goes:
time: 638 us; the launch traced here: 636 us
  waiting for transfers between devices  506 us (79%)
  matrix products  86.7 us (14%)
  local copies, waits for them, and re-layouts  18 us (3%)
  between operations  13.9 us (2%)
  other arithmetic  9.99 us (2%)
    reduce_scatter x1, waiting for transfers between devices, per_device(): lax.psum_scatter(lax.dot_general(cols, owned, contract, precision=exact,...  159 us
    reduce_scatter x1, waiting for transfers between devices, per_device(): lax.psum_scatter(partials.reshape(seq_len, 2 * head_dim), 'ctx', scatter_...  132 us
    unnamed x6, waiting for transfers between devices  99.2 us
    all_gather x1, waiting for transfers between devices, per_device(): lax.all_gather(values[0], 'ctx', axis=0, tiled=True)  59.7 us
    all_gather x1, waiting for transfers between devices, per_device(): lax.all_gather(keys[0], 'ctx', axis=0, tiled=True)  56.2 us
    dot_general x16, matrix products, scores(): jnp.einsum('thd,kd->htk', q_heads, kblock, preferred_element_type=jnp.flo...  23.5 us
    dot_general x16, matrix products, prob_grads(): jnp.einsum('thd,kd->htk', d_heads, vblock, preferred_element_type=jnp.flo...  23.1 us
    dot_general x8, matrix products, grad_step(): jnp.einsum('htk,kd->thd', dscore, kblock, preferred_element_type=jnp.floa...  18.3 us
  transfers between devices with their start and end apart: 5, of which 5 were waited for; matrix products, arithmetic and copies ran while one was open for 1% of the time, Pallas kernels for 0%

commit v1 on v0

--- a/solution.py
+++ b/solution.py
@@ -26,7 +26,9 @@
     local_rows = layer_input[0]
     all_keys, all_values = (
         lax.all_gather(keys[0], "ctx", axis=0, tiled=True),
-        lax.all_gather(values[0], "ctx", axis=0, tiled=True),
+        jnp.concatenate(
+            lax.all_to_all(jnp.stack([values[0]] * lax.axis_size("ctx")), "ctx", 0, 0), axis=0
+        ),
     )
     block = 512
     nblocks = seq_len // block

time: 638 us -> 581 us (0.911)
  waiting for transfers between devices: 506 us -> 442 us
  starting transfers between devices: 0.2 us -> 9.36 us
    all_gather x1 -> x0, waiting for transfers between devices: 59.7 us -> none  [per_device(): lax.all_gather(values[0], 'ctx', axis=0, tiled=True)]
    all_to_all x0 -> x1, starting transfers between devices: none -> 9.19 us  [per_device(): lax.all_to_all(jnp.stack([values[0]] * lax.axis_size('ctx')), 'ctx', 0, 0)]
    unnamed x6 -> x5, waiting for transfers between devices: 99.2 us -> 98.6 us
  transfers between devices with their start and end apart: 5 -> 5, of which waited for: 5 -> 4; matrix products, arithmetic and copies ran while one was open for 1% -> 1% of each run, Pallas kernels for 0% -> 0%
where the time goes in v1:
time: 581 us; the launch traced here: 580 us
  waiting for transfers between devices  442 us (76%)
  matrix products  86.6 us (15%)
  local copies, waits for them, and re-layouts  18.1 us (3%)
  between operations  13.9 us (2%)
  starting transfers between devices  9.36 us (2%)
  other arithmetic  8.69 us (1%)
    reduce_scatter x1, waiting for transfers between devices, per_device(): lax.psum_scatter(lax.dot_general(cols, owned, contract, precision=exact,...  159 us
    reduce_scatter x1, waiting for transfers between devices, per_device(): lax.psum_scatter(partials.reshape(seq_len, 2 * head_dim), 'ctx', scatter_...  132 us
    unnamed x5, waiting for transfers between devices  98.6 us
    all_gather x1, waiting for transfers between devices, per_device(): lax.all_gather(keys[0], 'ctx', axis=0, tiled=True)  52.6 us
    dot_general x16, matrix products, scores(): jnp.einsum('thd,kd->htk', q_heads, kblock, preferred_element_type=jnp.flo...  23.5 us
    dot_general x16, matrix products, prob_grads(): jnp.einsum('thd,kd->htk', d_heads, vblock, preferred_element_type=jnp.flo...  23.1 us
    dot_general x8, matrix products, grad_step(): jnp.einsum('htk,kd->thd', dscore, kblock, preferred_element_type=jnp.floa...  18.2 us
  transfers between devices with their start and end apart: 5, of which 4 were waited for; matrix products, arithmetic and copies ran while one was open for 1% of the time, Pallas kernels for 0%

profile of v1, /device:TPU:8, one launch (start us, length us, event | category | flops | bytes accessed | tf_op | source)
XLA Modules:
  0.0 579.9 jit_solution(1777726183831004694)
XLA Ops:
  8.0 2.0 stack.3
  10.0 9.2 %all-to-all-start = ((bf16[32,128,128]{2,1,0:T(8,128)(2,1)}), bf16[32,128,128]{2,1,0:T(8,128)(2,1)}, u32[]{:S(2)}, u32[]{:S(2)}) async-start(bf16[32,128,128]{2,1,0:T(8,128)(2,1)} %stack.3), calls=%async_computation | async-start | bytes 2097152 | tf_op jit(solution)/shard_map/all_to_all | solution.py:30
  22.6 52.6 %all-gather.3.cloned.1.call-done = bf16[1,4096,128]{2,1,0:T(8,128)(2,1)} async-done(((bf16[1,128,128]{2,1,0:T(8,128)(2,1)}), bf16[1,4096,128]{2,1,0:T(8,128)(2,1)}) %all-gather.3.cloned.1.call-update) | async-done | bytes 1048592 | tf_op jit(solution)/shard_map/all_gather | solution.py:28
  75.2 29.4 %while.28 = (s32[]{:T(128)}, f32[8,128]{1,0:T(8,128)S(1)}, f32[8,128]{1,0:T(8,128)S(1)}, f32[8,128]{1,0:T(8,128)S(1)}, s32[8,512]{1,0:T(8,128)S(1)}, /*index=5*/...) while((s32[]{:T(128)}, f32[8,128]{1,0:T(8,128)S(1)}, ...), condition=%wide.region_6.7_spmd.clone, body=%wide.region_2.6_spmd.clone.sunk | while | flops 274930688 | bytes 7427236 | solution.py:68
  76.8 1.6 fusion.66
  80.5 1.6 fusion.66
  84.2 1.6 fusion.66
  87.8 1.6 fusion.66
  91.5 1.6 fusion.66
  95.2 1.6 fusion.66
  104.6 67.3 %while.29 = (s32[]{:T(128)}, f32[128,8,128]{0,2,1:T(8,128)}, f32[8,512,256]{2,1,0:T(8,128)}, bf16[8,512,128]{2,1,0:T(8,128)(2,1)}, s32[8,512]{1,0:T(8,128)S(1)},...) while((s32[]{:T(128)}, f32[128,8,128]{0,2,1:T(8,128)}, ...), condition=%wide.region_8.9_spmd.clone, body=%wide.region_7.8_spmd.clone.sunk | while | flops 675414016 | bytes 15750323 | solution.py:87
  104.8 1.6 fusion.79
  109.7 2.1 fusion.81
  113.1 1.6 fusion.79
  117.9 2.3 fusion.81
  121.5 1.6 fusion.79
  126.3 2.3 fusion.81
  129.9 1.6 fusion.79
  134.8 2.3 fusion.81
  138.4 1.6 fusion.79
  143.2 2.3 fusion.81
  146.8 1.6 fusion.79
  151.6 2.3 fusion.81
  155.3 1.6 fusion.79
  160.1 2.3 fusion.81
  163.7 1.6 fusion.79
  168.5 2.3 fusion.81
  172.0 132.1 %reduce-scatter.6.cloned.1.call-done = f32[128,256]{1,0:T(8,128)} async-done(((f32[4096,256]{1,0:T(8,128)}), f32[128,256]{1,0:T(8,128)}) %reduce-scatter.6.cloned.1.call-update) | async-done | bytes 131088 | tf_op jit(solution)/shard_map/reduce_scatter | solution.py:90
  304.1 6.5 %convolution_bitcast_fusion.3 = f32[8192,256]{0,1:T(8,128)} fusion(f32[128,256]{1,0:T(8,128)} %reduce-scatter.6.cloned.1.call-done, bf16[1,128,8192]{2,1,0:T(8,128)(2,1)S(1)} %copy-done), kind=kOutput, calls=%fused_computation.50 | convolution fusion | flops 3221225472 | bytes 10616832 | tf_op jit(solution)/shard_map/dot_general | solution.py:99
  310.7 158.8 %reduce-scatter.8.cloned.1.call-done = f32[256,256]{0,1:T(8,128)} async-done(((f32[8192,256]{0,1:T(8,128)}), f32[256,256]{0,1:T(8,128)}) %reduce-scatter.8.cloned.1.call-update) | async-done | bytes 262160 | tf_op jit(solution)/shard_map/reduce_scatter | solution.py:98
  469.5 1.8 copy.58
  473.9 97.9 %reduce-scatter.10.cloned.1.call-done = f32[32,256]{1,0:T(8,128)} async-done(((f32[256,256]{1,0:T(8,128)}), f32[32,256]{1,0:T(8,128)}) %reduce-scatter.10.cloned.1.call-update) | async-done | bytes 32784
  (174 shorter events, 63.8 us)
Async XLA Ops:
  7.2 296.9 %copy-start = (bf16[1,128,8192]{2,1,0:T(8,128)(2,1)S(1)}, bf16[1,128,8192]{2,1,0:T(8,128)(2,1)}, u32[]{:S(2)}) copy-start(bf16[1,128,8192]{2,1,0:T(8,128)(2,1)} %param.11) | copy-start | bytes 6291460
  7.2 12.1 %copy-start.4 = (s32[1,8]{1,0:T(1,128)S(1)}, s32[1,8]{1,0:T(1,128)}, u32[]{:S(2)}) copy-start(s32[1,8]{1,0:T(1,128)} %param.16) | copy-start | bytes 100
  7.2 12.3 %copy-start.5 = (s32[64]{0:T(128)S(1)}, s32[64]{0:T(128)}, u32[]{:S(2)}) copy-start(s32[64]{0:T(128)} %param.17) | copy-start | bytes 772
  7.2 13.0 %copy-start.2 = (bf16[1,128,1024]{2,1,0:T(8,128)(2,1)S(1)}, bf16[1,128,1024]{2,1,0:T(8,128)(2,1)}, u32[]{:S(2)}) copy-start(bf16[1,128,1024]{2,1,0:T(8,128)(2,1)} %param.12) | copy-start | bytes 786436
  7.2 68.0 %all-gather.3.cloned.1.call-start = ((), (), s32[]{:S(2)}) async-start(), calls=%async_computation.6 | async-start | bytes 1081344 | tf_op jit(solution)/shard_map/all_gather | solution.py:28
  7.9 14.3 %copy-start.3 = (bf16[1,128,1024]{2,1,0:T(8,128)(2,1)S(1)}, bf16[1,128,1024]{2,1,0:T(8,128)(2,1)}, u32[]{:S(2)}) copy-start(bf16[1,128,1024]{2,1,0:T(8,128)(2,1)} %param.15) | copy-start | bytes 786436
  10.0 65.2 %all-to-all-start = ((bf16[32,128,128]{2,1,0:T(8,128)(2,1)}), bf16[32,128,128]{2,1,0:T(8,128)(2,1)}, u32[]{:S(2)}, u32[]{:S(2)}) async-start(bf16[32,128,128]{2,1,0:T(8,128)(2,1)} %stack.3), calls=%async_computation | async-start | bytes 2097152 | tf_op jit(solution)/shard_map/all_to_all | solution.py:30
  19.2 284.9 %reduce-scatter.6.cloned.1.call-start = ((), (), s32[]{:S(2)}) async-start(), calls=%async_computation.4 | async-start | bytes 4325376 | tf_op jit(solution)/shard_map/reduce_scatter | solution.py:90
  171.9 297.6 %reduce-scatter.8.cloned.1.call-start = ((), (), s32[]{:S(2)}) async-start(), calls=%async_computation.5 | async-start | bytes 8650752 | tf_op jit(solution)/shard_map/reduce_scatter | solution.py:98
  310.7 162.6 %copy-start.1 = (f32[128,256]{1,0:T(8,128)S(1)}, f32[128,256]{1,0:T(8,128)}, u32[]{:S(2)}) copy-start(f32[128,256]{1,0:T(8,128)} %reduce-scatter.6.cloned.1.call-done) | copy-start | bytes 393220
  310.7 261.2 %reduce-scatter.10.cloned.1.call-start = ((), (), s32[]{:S(2)}) async-start(), calls=%async_computation.7 | async-start | bytes 294912
Sparse Core Ops, SparseCore 0:
  9.9 65.2 all-gather.2
  172.1 131.9 reduce-scatter.5
  310.8 158.7 reduce-scatter.7
  473.2 98.5 reduce-scatter.9
